TPU v7x, 32 devices: a whole 2x2x4 slice. The times are simulated.
32 devices in a mesh: groups: 2 (over y), tm: 4 (over z), space: 2 (over x), mp: 2 (over core).
Axes of the slice: x: 2, y: 2, z: 4, core: 2. Of those that a mesh axis runs over, the one named last changes fastest.
Arguments:
- query_proj: bfloat16 [16, 16, 8, 2240], P(('groups', 'tm'), 'space', None, 'mp'), parts along dimension 0, may hold values from -6 to 6
- key_proj: bfloat16 [16, 16, 8, 2240], P(('groups', 'tm'), 'space', None, 'mp'), parts along dimension 0, may hold values from -6 to 6
- value_proj: bfloat16 [16, 16, 8, 2240], P(('groups', 'tm'), 'space', None, 'mp'), parts along dimension 0, may hold values from -6 to 6
- expanded: bfloat16 [16, 16, 8, 2, 6720], P(('groups', 'tm'), 'space', None, None, 'mp'), parts along dimension 0, may hold values from -6 to 6
- spatial_weight: float32 [3, 3, 2, 6720], P(None, None, None, 'mp'), may hold values from -0.6 to 0.6
- temporal_weight: float32 [3, 2, 6720], P(None, None, 'mp'), may hold values from -1 to 1
Outputs:
- attended: bfloat16 [16, 16, 8, 2240], P(('groups', 'tm'), 'space', None, 'mp'), parts along dimension 0
- gated_hidden: bfloat16 [16, 16, 8, 6720], P(('groups', 'tm'), 'space', None, 'mp'), parts along dimension 0
There are 2 independent parts, one for each index of `groups`. A program takes and returns all parts, laid end to end along the dimension named above; an argument that names none is the same for every part. Nothing has to cross between parts.
All inputs are finite; a program needn't handle non-finite values.
Results may differ from a plain program's by a relative error of at most 0.0059.
Values may be sent and summed in bfloat16 or wider, within the bound.
A program may use at most 64 MiB of HBM per device.

v0:
```python
import jax
import jax.numpy as jnp
from jax import lax
from jax.sharding import PartitionSpec as P

HEAD_DIM = 32


def carried_in(value, axis, join, neutral):
    count, mine = (lax.axis_size(axis), lax.axis_index(axis))
    pieces = jax.tree.map(lambda part: lax.all_gather(part, axis), value)
    so_far = jax.tree.map(
        lambda part, zero: jnp.full_like(part, 0) + jnp.asarray(zero, part.dtype), value, neutral
    )

    def turn(position, so_far):
        longer = join(so_far, jax.tree.map(lambda part: part[position], pieces))
        return jax.tree.map(lambda new, old: jnp.where(position < mine, new, old), longer, so_far)

    return lax.fori_loop(0, count - 1, turn, so_far)


def padded_2(cells, sides, width):
    for axis, dim in sides:
        count = lax.axis_size(axis)
        ends = count - 1
        head = lax.slice_in_dim(cells, 0, width, axis=dim)
        tail = lax.slice_in_dim(cells, cells.shape[dim] - width, cells.shape[dim], axis=dim)
        cells = jnp.concatenate(
            [
                lax.ppermute(tail, axis, [(i, (i + 1) % count) for i in range(ends)]),
                cells,
                lax.ppermute(head, axis, [((i + 1) % count, i) for i in range(ends)]),
            ],
            axis=dim,
        )
    return cells


def passed_along(value, axis, steps):
    count = lax.axis_size(axis)
    first, last = (max(0, -steps), min(count, count - steps))
    return lax.ppermute(value, axis, [(source, source + steps) for source in range(first, last)])


def add_states(first_pair, second_pair):
    return (first_pair[0] + second_pair[0], first_pair[1] + second_pair[1])


def earlier_states(states):
    empty = (jnp.zeros_like(states[0]), jnp.zeros_like(states[1]))
    return carried_in(states, "tm", add_states, empty)


def conv_block(extended, spatial_weight):
    row_count = extended.shape[1] - 2
    col_count = extended.shape[2]
    padded = jnp.pad(extended, ((0, 0), (0, 0), (1, 1), (0, 0), (0, 0)))
    summed = jnp.zeros((extended.shape[0], row_count, col_count) + extended.shape[3:], jnp.float32)
    for row_tap in range(3):
        for col_tap in range(3):
            summed = (
                summed
                + padded[:, row_tap : row_tap + row_count, col_tap : col_tap + col_count].astype(
                    jnp.float32
                )
                * spatial_weight[row_tap, col_tap]
            )
    return summed.astype(jnp.bfloat16)


def on_device(query_proj, key_proj, value_proj, expanded, spatial_weight, temporal_weight):
    frames = query_proj.shape[0]
    row_count = query_proj.shape[1]
    col_count = query_proj.shape[2]
    channels = query_proj.shape[3]
    head_count = channels // HEAD_DIM
    key_relu = jnp.maximum(key_proj, 0).reshape(-1, head_count, HEAD_DIM)
    value_rows = value_proj.reshape(-1, head_count, HEAD_DIM)
    kv_state = jnp.einsum(
        "thd,the->dhe", key_relu, value_rows, preferred_element_type=jnp.float32
    ).reshape(HEAD_DIM, channels)
    key_sum = jnp.sum(key_relu.astype(jnp.float32), axis=0).reshape(channels)
    local_states = (kv_state, key_sum)
    before = earlier_states(local_states)
    combined = lax.psum(add_states(before, local_states), "space")
    query_relu = jnp.maximum(query_proj, 0).reshape(-1, head_count, HEAD_DIM).astype(jnp.float32)
    numerator = jnp.einsum(
        "thd,dhe->the",
        query_relu,
        combined[0].reshape(HEAD_DIM, head_count, HEAD_DIM),
        precision=lax.Precision.HIGHEST,
    )
    denominator = (
        jnp.einsum(
            "thd,hd->th",
            query_relu,
            combined[1].reshape(head_count, HEAD_DIM),
            precision=lax.Precision.HIGHEST,
        )
        + 1.0
    )
    attended = (
        (numerator / denominator[..., None])
        .reshape(frames, row_count, col_count, channels)
        .astype(jnp.bfloat16)
    )
    extended = padded_2(expanded, (("space", 1),), 1)
    spatial = conv_block(extended, spatial_weight)
    earlier_frames = passed_along(spatial, "tm", 1)
    timeline = jnp.concatenate([earlier_frames, spatial], axis=0)
    mixed = (
        timeline[:-2].astype(jnp.float32) * temporal_weight[0]
        + timeline[1:-1].astype(jnp.float32) * temporal_weight[1]
        + timeline[2:].astype(jnp.float32) * temporal_weight[2]
    )
    gated_hidden = (mixed[..., 0, :] * jax.nn.silu(mixed[..., 1, :])).astype(jnp.bfloat16)
    return (attended, gated_hidden)


def solution(mesh):
    return jax.shard_map(
        on_device,
        mesh=mesh,
        in_specs=(
            P(("groups", "tm"), "space", None, "mp"),
            P(("groups", "tm"), "space", None, "mp"),
            P(("groups", "tm"), "space", None, "mp"),
            P(("groups", "tm"), "space", None, None, "mp"),
            P(None, None, None, "mp"),
            P(None, None, "mp"),
        ),
        out_specs=(
            P(("groups", "tm"), "space", None, "mp"),
            P(("groups", "tm"), "space", None, "mp"),
        ),
        check_vma=False,
    )
```

profile of v0, /device:TPU:0, one launch (start us, length us, event | category | flops | bytes accessed | tf_op | source)
XLA Modules:
  0.0 113.3 jit_solution(13310139821514599711)
XLA Ops:
  7.2 1.7 %copy.39 = bf16[2,8,8,2,3360]{4,2,1,0,3:T(8,128)(2,1)S(1)} copy(bf16[2,8,8,2,3360]{4,3,2,1,0:T(2,128)(2,1)} %param.11) | data formatting | bytes 3440640 | tf_op args[3]
  8.9 0.8 fusion.15
  9.7 5.5 %collective-permute-start = (bf16[2,1,8,2,3360]{4,2,1,0,3:T(8,128)(2,1)}, bf16[2,1,8,2,3360]{4,2,1,0,3:T(8,128)(2,1)}, u32[]{:S(2)}, u32[]{:S(2)}) collective-permute-start(bf16[2,1,8,2,3360]{4,2,1,0,3:T(8,128)(2,1)} %get-tuple-element.149), channel_id=1, source_target_pairs={{0,2},{1,3},{4,6},{5,7},{8,10},{9,11},{12,14},{13,15},{16,18},{17,... | collective-permute-start | bytes 645128 | tf_op jit(solution)/shard_map/ppermute | solution.py:31
  15.2 1.3 %collective-permute-start.1 = (bf16[2,1,8,2,3360]{4,2,1,0,3:T(8,128)(2,1)}, bf16[2,1,8,2,3360]{4,2,1,0,3:T(8,128)(2,1)}, u32[]{:S(2)}, u32[]{:S(2)}) collective-permute-start(bf16[2,1,8,2,3360]{4,2,1,0,3:T(8,128)(2,1)} %get-tuple-element.150), channel_id=1, source_target_pairs={{2,0},{3,1},{6,4},{7,5},{10,8},{11,9},{14,12},{15,13},{18,16},{19,... | collective-permute-start | bytes 645128 | tf_op jit(solution)/shard_map/ppermute | solution.py:33
  16.7 1.0 reshape.41
  17.7 2.7 %reshape.42 = bf16[128,35,32]{2,1,0:T(8,128)(2,1)} reshape(bf16[2,8,8,1120]{3,2,1,0:T(8,128)(2,1)} %param.10) | data formatting | bytes 573440 | tf_op jit(solution)/shard_map/reshape | solution.py:79
  20.4 1.8 %convolution_bitcast_fusion.1 = f32[32,35,32]{2,0,1:T(8,128)S(1)} fusion(bf16[128,35,32]{2,1,0:T(8,128)(2,1)} %reshape.42, bf16[128,35,32]{2,1,0:T(8,128)(2,1)S(1)} %reshape.41), kind=kOutput, calls=%fused_computation.21 | convolution fusion | flops 9175040 | bytes 716800 | tf_op jit(solution)/shard_map/thd,the->dhe/dot_general | solution.py:80
  22.9 0.6 dynamic-slice
  24.5 19.1 %all-reduce.1 = f32[4480]{0:T(1024)S(1)} all-reduce(f32[4480]{0:T(1024)S(1)} %dynamic-update-slice), channel_id=2, replica_groups=mesh['groups'=2,'tm'=4,'space'=2,'mp'=2] {'tm'}, use_global_device_ids=true, to_apply=%add.1 | all-reduce | flops 4480 | bytes 35840
  43.7 15.4 %all_gather.6 = f32[4,32,1120]{2,1,0:T(8,128)S(1)} all-gather(f32[1,32,1120]{2,1,0:T(8,128)S(1)} %all_gather_reshape.6), channel_id=1, replica_groups=mesh['groups'=2,'tm'=4,'space'=2,'mp'=2] {'tm'}, dimensions={0}, use_global_device_ids=true | all-gather | bytes 716800 | tf_op jit(solution)/shard_map/all_gather | solution.py:11
  59.4 1.0 copy.36
  60.6 2.7 %fusion.5 = bf16[2,10,10,2,3360]{4,2,1,0,3:T(8,128)(2,1)S(1)} fusion(bf16[2,1,8,2,3360]{4,2,1,0,3:T(8,128)(2,1)} %collective-permute-done.1, bf16[2,8,8,2,3360]{4,2,1,0,3:T(8,128)(2,1)S(1)} %copy.39, bf16[2,1,8,2,3360]{4,2,1,0,3:T(8,128)(2,1)} %collective-permute-done), kind=kLoop, calls=%fused_computation.10 | loop fusion | flops 16128000 | bytes 4838400 | tf_op jit(solution)/shard_map/concatenate | solution.py:29
  63.3 5.1 %add_convert_fusion = bf16[2,8,8,2,3360]{4,2,1,0,3:T(8,128)(2,1)S(1)} fusion(bf16[2,8,8,2,3360]{4,2,1,0,3:T(8,128)(2,1)S(1)} %copy.39, bf16[2,10,10,2,3360]{4,2,1,0,3:T(8,128)(2,1)S(1)} %fusion.5, bf16[2,1,8,2,3360]{4,2,1,0,3:T(8,128)(2,1)} %collective-permute-done.1, bf16[2,1,8,2,3360]{4,2,1,0,3:T(8,128)(2,1)} %collective-permute-done, ...), kind=kLoop, calls=%fused_computation.12 | loop fusion | flops 24944640 | bytes 14434560 | tf_op jit(solution)/shard_map/convert_element_type | solution.py:69
  68.4 2.7 %collective-permute-start.2 = (bf16[2,8,8,2,3360]{4,2,1,0,3:T(8,128)(2,1)S(1)}, bf16[2,8,8,2,3360]{4,2,1,0,3:T(8,128)(2,1)}, u32[]{:S(2)}, u32[]{:S(2)}) collective-permute-start(bf16[2,8,8,2,3360]{4,2,1,0,3:T(8,128)(2,1)S(1)} %add_convert_fusion), channel_id=1, source_target_pairs={{0,4},{4,8},{8,12},{1,5},{5,9},{9,13},{2,6},{6,10},{10,14},{3,7},{... | collective-permute-start | bytes 5160968 | tf_op jit(solution)/shard_map/ppermute | solution.py:43
  71.2 1.0 reshape.45
  72.2 1.5 %copy.37 = bf16[128,35,32]{0,2,1:T(8,128)(2,1)S(1)} copy(bf16[128,35,32]{2,1,0:T(8,128)(2,1)S(1)} %reshape.45) | data formatting | bytes 573440 | tf_op jit(solution)/shard_map/reshape | solution.py:87
  73.7 10.7 %psum.15 = f32[35,32]{1,0:T(8,128)S(1)} all-reduce(f32[35,32]{1,0:T(8,128)S(1)} %reshape.46), channel_id=1, replica_groups=mesh['groups'=2,'tm'=4,'space'=2,'mp'=2] {'space'}, use_global_device_ids=true, to_apply=%region_4.5 | all-reduce | flops 1120 | bytes 8960 | tf_op jit(solution)/shard_map/psum | solution.py:86
  84.8 6.7 %all-reduce.4.cloned.1.call-done = f32[32,35,32]{0,2,1:T(8,128)} async-done(((f32[32,35,32]{0,2,1:T(8,128)}), f32[32,35,32]{0,2,1:T(8,128)}) %all-reduce.4.cloned.1.call-update) | async-done | bytes 143376 | tf_op jit(solution)/shard_map/psum | solution.py:86
  91.5 2.2 %fusion.9 = bf16[128,35,32]{0,2,1:T(8,128)(2,1)} fusion(f32[32,35,32]{0,2,1:T(8,128)} %all-reduce.4.cloned.1.call-done, bf16[128,35,32]{0,2,1:T(8,128)(2,1)S(1)} %copy.37, f32[128,35]{0,1:T(8,128)S(1)} %fusion.12), kind=kOutput, calls=%fused_computation.23 | convolution fusion | flops 55336960 | bytes 734720 | tf_op jit(solution)/shard_map/thd,dhe->the/dot_general | solution.py:88
  93.6 1.9 %copy.38 = bf16[128,35,32]{2,1,0:T(8,128)(2,1)S(1)} copy(bf16[128,35,32]{0,2,1:T(8,128)(2,1)} %fusion.9) | data formatting | bytes 573440 | tf_op jit(solution)/shard_map/convert_element_type | solution.py:106
  95.6 1.4 %convert_element_type.57 = bf16[2,8,8,1120]{3,2,1,0:T(8,128)(2,1)} reshape(bf16[128,35,32]{2,1,0:T(8,128)(2,1)S(1)} %copy.38) | data formatting | bytes 573440 | tf_op jit(solution)/shard_map/convert_element_type | solution.py:106
  96.9 5.4 %collective-permute-done.2 = bf16[2,8,8,2,3360]{4,2,1,0,3:T(8,128)(2,1)} collective-permute-done((bf16[2,8,8,2,3360]{4,2,1,0,3:T(8,128)(2,1)S(1)}, bf16[2,8,8,2,3360]{4,2,1,0,3:T(8,128)(2,1)}, u32[]{:S(2)}, u32[]{:S(2)}) %collective-permute-start.2) | collective-permute-done | bytes 1720352 | tf_op jit(solution)/shard_map/ppermute | solution.py:43
  102.4 2.6 %multiply_add_fusion = f32[2,8,8,2,3360]{4,2,1,0,3:T(8,128)S(1)} fusion(bf16[2,8,8,2,3360]{4,2,1,0,3:T(8,128)(2,1)S(1)} %add_convert_fusion, bf16[2,8,8,2,3360]{4,2,1,0,3:T(8,128)(2,1)} %collective-permute-done.2, f32[2,3360]{1,0:T(2,128)S(1)} %get-tuple-element.161, f32[2,3360]{1,0:T(2,128)S(1)} %get-tuple-element.162, f32[2,3360]{1,0:T(2,128)S(1)} %get-tuple-element.160), kind=kLoop, calls=%fused_computation.11 | loop fusion | flops 7741440 | bytes 6961920 | tf_op jit(solution)/shard_map/add | solution.py:113
  105.0 1.4 %fusion.7 = bf16[2,8,8,3360]{3,2,1,0:T(8,128)(2,1)} fusion(f32[2,8,8,2,3360]{4,2,1,0,3:T(8,128)S(1)} %multiply_add_fusion), kind=kLoop, calls=%fused_computation.16 | loop fusion | flops 2580480 | bytes 4300800 | tf_op jit(solution)/shard_map/convert_element_type | solution.py:117
  (42 shorter events, 2.3 us)
Async XLA Ops:
  7.2 9.4 %copy-start = (bf16[2,8,8,1120]{3,2,1,0:T(8,128)(2,1)S(1)}, bf16[2,8,8,1120]{3,2,1,0:T(8,128)(2,1)}, u32[]{:S(2)}) copy-start(bf16[2,8,8,1120]{3,2,1,0:T(8,128)(2,1)} %param.9) | copy-start | bytes 860164
  7.2 84.3 %all-reduce.4.cloned.1.call-start = ((), (), s32[]{:S(2)}) async-start(), calls=%async_computation | async-start | bytes 1146880 | tf_op jit(solution)/shard_map/psum | solution.py:86
  9.7 50.8 %collective-permute-start = (bf16[2,1,8,2,3360]{4,2,1,0,3:T(8,128)(2,1)}, bf16[2,1,8,2,3360]{4,2,1,0,3:T(8,128)(2,1)}, u32[]{:S(2)}, u32[]{:S(2)}) collective-permute-start(bf16[2,1,8,2,3360]{4,2,1,0,3:T(8,128)(2,1)} %get-tuple-element.149), channel_id=1, source_target_pairs={{0,2},{1,3},{4,6},{5,7},{8,10},{9,11},{12,14},{13,15},{16,18},{17,... | collective-permute-start | bytes 645128 | tf_op jit(solution)/shard_map/ppermute | solution.py:31
  15.2 45.3 %collective-permute-start.1 = (bf16[2,1,8,2,3360]{4,2,1,0,3:T(8,128)(2,1)}, bf16[2,1,8,2,3360]{4,2,1,0,3:T(8,128)(2,1)}, u32[]{:S(2)}, u32[]{:S(2)}) collective-permute-start(bf16[2,1,8,2,3360]{4,2,1,0,3:T(8,128)(2,1)} %get-tuple-element.150), channel_id=1, source_target_pairs={{2,0},{3,1},{6,4},{7,5},{10,8},{11,9},{14,12},{15,13},{18,16},{19,... | collective-permute-start | bytes 645128 | tf_op jit(solution)/shard_map/ppermute | solution.py:33
  17.6 5.3 %copy-start.4 = (u32[32]{0:T(128)S(1)}, u32[32]{0:T(128)}, u32[]{:S(2)}) copy-start(u32[32]{0:T(128)} %constant.48) | copy-start | bytes 388
  22.5 38.0 %copy-start.2 = (f32[3,3,2,3360]{3,2,1,0:T(2,128)S(1)}, f32[3,3,2,3360]{3,2,1,0:T(2,128)}, u32[]{:S(2)}) copy-start(f32[3,3,2,3360]{3,2,1,0:T(2,128)} %param.12) | copy-start | bytes 725764
  63.3 7.8 %copy-start.1 = (bf16[2,8,8,1120]{3,2,1,0:T(8,128)(2,1)S(1)}, bf16[2,8,8,1120]{3,2,1,0:T(8,128)(2,1)}, u32[]{:S(2)}) copy-start(bf16[2,8,8,1120]{3,2,1,0:T(8,128)(2,1)} %param.8) | copy-start | bytes 860164
  68.4 16.3 %copy-start.3 = (f32[3,2,3360]{2,1,0:T(2,128)S(1)}, f32[3,2,3360]{2,1,0:T(2,128)}, u32[]{:S(2)}) copy-start(f32[3,2,3360]{2,1,0:T(2,128)} %param.13) | copy-start | bytes 241924
  68.4 34.0 %collective-permute-start.2 = (bf16[2,8,8,2,3360]{4,2,1,0,3:T(8,128)(2,1)S(1)}, bf16[2,8,8,2,3360]{4,2,1,0,3:T(8,128)(2,1)}, u32[]{:S(2)}, u32[]{:S(2)}) collective-permute-start(bf16[2,8,8,2,3360]{4,2,1,0,3:T(8,128)(2,1)S(1)} %add_convert_fusion), channel_id=1, source_target_pairs={{0,4},{4,8},{8,12},{1,5},{5,9},{9,13},{2,6},{6,10},{10,14},{3,7},{... | collective-permute-start | bytes 5160968 | tf_op jit(solution)/shard_map/ppermute | solution.py:43
Sparse Core Ops, SparseCore 0:
  60.6 30.7 all-reduce.3
where the time goes:
time: 115 us; the launch traced here: 113 us
  blocking collectives  45.3 us (39%)
  local copies, waits for them, and re-layouts  14.9 us (13%)
  between operations  14.9 us (13%)
  other arithmetic  12.2 us (11%)
  waiting for transfers between devices  12.1 us (11%)
  starting transfers between devices  9.5 us (8%)
  matrix products  4.28 us (4%)
    unnamed x1, blocking collectives  19.1 us
    all_gather x1, blocking collectives, carried_in(): pieces = jax.tree.map(lambda part: lax.all_gather(part, axis), value)  15.4 us
    psum x1, blocking collectives, on_device(): combined = lax.psum(add_states(before, local_states), 'space')  10.7 us
    psum x1, waiting for transfers between devices, on_device(): combined = lax.psum(add_states(before, local_states), 'space')  6.68 us
    ppermute x1, starting transfers between devices, padded_2(): lax.ppermute(tail, axis, [(i, (i + 1) % count) for i in range(ends)])  5.52 us
    ppermute x1, waiting for transfers between devices, passed_along(): lax.ppermute(value, axis, [(source, source + steps) for source in range(f...  5.45 us
    convert_element_type x1, other arithmetic, conv_block(): return summed.astype(jnp.bfloat16)  5.09 us
    convert_element_type x2, local copies, waits for them, and re-layouts, on_device(): attended = (numerator / denominator[..., None]).reshape(frames, row_count...  3.31 us
  transfers between devices with their start and end apart: 4, of which 2 were waited for; matrix products, arithmetic and copies ran while one was open for 22% of the time, Pallas kernels for 0%

commit v1 on v0

v1 whole, which is shorter than its diff:
```python
import functools

import jax
import jax.numpy as jnp
from jax import lax
from jax.experimental import pallas as pl
from jax.experimental.pallas import tpu as pltpu
from jax.sharding import PartitionSpec as P

HEAD_DIM = 32
LANES = 128
CHUNK = 3
ST = HEAD_DIM + 8
MESH = pl.DeviceIdType.MESH
F32 = jnp.float32
BF16 = jnp.bfloat16


def kernel(
    plan, q_ref, k_ref, v_ref, x_ref, sw_ref, tw_ref, att_ref, out_ref,
    spat, recv, outs, hsend, hrecv, state, rs_buf, prefix, pre_in, full,
    h_ss, h_rs, m_ss, m_rs, o_ss, o_rs, rs_ss, rs_rs, ag_ss, ag_rs, ch_ss, ch_rs,
):
    n_tm, n_sp, order, a_list, b_list = plan
    frames = x_ref.shape[1]
    cols = hsend.shape[2] // frames
    rows = x_ref.shape[2] // cols
    c = lax.axis_index("tm")
    s = lax.axis_index("space")
    has_prev, has_next = c > 0, c < n_tm - 1
    has_up, has_down = s > 0, s < n_sp - 1
    width = CHUNK * LANES

    def lanes(chunk):
        return pl.ds(chunk * width, width)

    def remote(src, dst, ss, rs, **where):
        return pltpu.make_async_remote_copy(
            src_ref=src, dst_ref=dst, send_sem=ss, recv_sem=rs,
            device_id=where, device_id_type=MESH,
        )

    def when(cond):
        return pl.when(cond)

    up_id, down_id = jnp.maximum(s - 1, 0), jnp.minimum(s + 1, n_sp - 1)
    prev_id, next_id = jnp.maximum(c - 1, 0), jnp.minimum(c + 1, n_tm - 1)

    barrier = pltpu.get_barrier_semaphore()
    for off in range(1, n_sp):
        pl.semaphore_signal(barrier, inc=1, device_id={"space": lax.rem(s + off, n_sp)}, device_id_type=MESH)

    @when(has_prev)
    def _():
        pl.semaphore_signal(barrier, inc=1, device_id={"tm": prev_id}, device_id_type=MESH)

    @when(has_next)
    def _():
        pl.semaphore_signal(barrier, inc=1, device_id={"tm": next_id}, device_id_type=MESH)

    n_tiles = x_ref.shape[3] // LANES

    def edges(t, _):
        at = pl.ds(pl.multiple_of(t * LANES, LANES), LANES)
        for vg in range(2):
            top = [x_ref[vg, f, 0 : 2 * cols, at].astype(F32)[:cols] for f in range(frames)]
            low = [x_ref[vg, f, (rows - 2) * cols : rows * cols, at].astype(F32)[cols:] for f in range(frames)]
            hsend[0, vg, :, at] = jnp.concatenate(top, axis=0).astype(BF16)
            hsend[1, vg, :, at] = jnp.concatenate(low, axis=0).astype(BF16)
        return 0

    lax.fori_loop(0, n_tiles, edges, 0)

    @when(jnp.logical_not(has_up))
    def _():
        hrecv[0] = jnp.zeros(hrecv.shape[1:], BF16)

    @when(jnp.logical_not(has_down))
    def _():
        hrecv[1] = jnp.zeros(hrecv.shape[1:], BF16)

    pl.semaphore_wait(barrier, n_sp - 1 + jnp.minimum(c, 1) + jnp.minimum(n_tm - 1 - c, 1))

    def halo(chunk, way):
        return remote(
            hsend.at[way, :, :, lanes(chunk)], hrecv.at[1 - way, :, :, lanes(chunk)],
            h_ss.at[way, chunk], h_rs.at[1 - way, chunk], space=up_id if way == 0 else down_id,
        )

    def halo_in(chunk, side):
        return remote(
            hsend.at[side, :, :, lanes(chunk)], hrecv.at[side, :, :, lanes(chunk)],
            h_ss.at[side, chunk], h_rs.at[side, chunk], space=up_id if side == 0 else down_id,
        )

    for chunk in order:
        for way, cond in ((0, has_up), (1, has_down)):
            when(cond)(lambda chunk=chunk, way=way: halo(chunk, way).start())

    channels = q_ref.shape[-1]
    heads_tiles = -(-channels // LANES)
    tokens = q_ref.shape[0]
    row_id = lax.broadcasted_iota(jnp.int32, (LANES, LANES), 0) // HEAD_DIM
    col_id = lax.broadcasted_iota(jnp.int32, (LANES, LANES), 1) // HEAD_DIM
    same = row_id == col_id

    def tile_of(ref, t):
        lo, hi = t * LANES, min(channels, (t + 1) * LANES)
        part = ref[:, lo:hi].astype(F32)
        if hi - lo < LANES:
            part = jnp.concatenate([part, jnp.zeros((tokens, LANES - hi + lo), F32)], axis=1)
        return part

    for t in range(heads_tiles):
        key = jnp.maximum(tile_of(k_ref, t), 0.0)
        kv = lax.dot_general(
            key.T.astype(BF16), tile_of(v_ref, t).astype(BF16),
            (((1,), (0,)), ((), ())), preferred_element_type=F32,
        )
        kv = jnp.where(same, kv, 0.0)
        small = kv[:HEAD_DIM]
        for j in range(1, LANES // HEAD_DIM):
            small = small + kv[j * HEAD_DIM : (j + 1) * HEAD_DIM]
        state[t, :HEAD_DIM] = small
        state[t, HEAD_DIM:] = jnp.broadcast_to(jnp.sum(key, axis=0, keepdims=True), (ST - HEAD_DIM, LANES))
    for t in range(heads_tiles, state.shape[0]):
        state[t] = jnp.zeros((ST, LANES), F32)

    per = state.shape[0] // n_sp

    def share(dev):
        return pl.ds(dev * per, per)

    def scatter(off):
        peer = lax.rem(s + off, n_sp)
        return remote(state.at[share(peer)], rs_buf.at[off - 1], rs_ss.at[off - 1], rs_rs.at[off - 1], space=peer)

    def gather(off):
        peer = lax.rem(s + off, n_sp)
        return remote(prefix, full.at[off - 1], ag_ss.at[off - 1], ag_rs.at[off - 1], space=peer)

    for off in range(1, n_sp):
        scatter(off).start()

    def chain():
        return remote(prefix, pre_in, ch_ss, ch_rs, tm=next_id)

    def hop():
        total = state[share(s)]
        for off in range(1, n_sp):
            total = total + rs_buf[off - 1]

        @when(has_prev)
        def _():
            chain().wait_recv()
            prefix[...] = total + pre_in[...]

        @when(jnp.logical_not(has_prev))
        def _():
            prefix[...] = total

        when(has_next)(lambda: chain().start())
        for off in range(1, n_sp):
            gather(off).start()

    col = lax.broadcasted_iota(jnp.int32, (cols, LANES), 0)

    def conv(chunk):
        def tile(t, _):
            at = pl.ds(pl.multiple_of(chunk * width + t * LANES, LANES), LANES)
            for vg in range(2):
                taps = []
                for a in range(3):
                    for b in range(3):
                        w = jnp.broadcast_to(sw_ref[a, b, vg : vg + 1, at], (cols, LANES))
                        if b == 0:
                            w = jnp.where(col == 0, 0.0, w)
                        if b == 2:
                            w = jnp.where(col == cols - 1, 0.0, w)
                        taps.append(w[None])
                above = hrecv[0, vg, :, at].astype(F32).reshape(frames, 1, cols, LANES)
                below = hrecv[1, vg, :, at].astype(F32).reshape(frames, 1, cols, LANES)
                for f in range(frames):
                    body = x_ref[vg, f, :, at].astype(F32).reshape(rows, cols, LANES)
                    ext = jnp.concatenate([above[f], body, below[f]], axis=0)
                    moved = [pltpu.roll(ext, 1, 1), ext, pltpu.roll(ext, cols - 1, 1)]
                    total = None
                    for a in range(3):
                        for b in range(3):
                            term = moved[b][a : a + rows] * taps[3 * a + b]
                            total = term if total is None else total + term
                    spat[vg, f, :, at] = total.reshape(rows * cols, LANES).astype(BF16)
            return 0

        lax.fori_loop(0, CHUNK, tile, 0)

    def gate(chunk, before, now, into):
        def tile(t, _):
            at = pl.ds(pl.multiple_of(chunk * width + t * LANES, LANES), LANES)
            mixed = []
            for vg in range(2):
                w = [tw_ref[j, vg : vg + 1, at] for j in range(3)]
                line = [now[vg, f, :, at].astype(F32) for f in range(frames)]
                if before is not None:
                    line = [before[vg, f, :, at].astype(F32) for f in (frames - 2, frames - 1)] + line
                    mixed.append([line[f] * w[0] + line[f + 1] * w[1] + line[f + 2] * w[2] for f in range(frames)])
                else:
                    got = []
                    for f in range(frames):
                        m = line[f] * w[2]
                        if f >= 1:
                            m = line[f - 1] * w[1] + m
                        if f >= 2:
                            m = line[f - 2] * w[0] + m
                        got.append(m)
                    mixed.append(got)
            for f in range(frames):
                v, g = mixed[0][f], mixed[1][f]
                into[f, :, at] = (v * (g / (1.0 + jnp.exp(-g)))).astype(BF16)
            return 0

        lax.fori_loop(0, CHUNK, tile, 0)

    def ahead(chunk):
        part = (slice(None), slice(None), slice(None), lanes(chunk))
        return remote(spat.at[part], recv.at[part], m_ss.at[chunk], m_rs.at[chunk], tm=next_id)

    def back(chunk):
        part = (slice(None), slice(None), slice(None), lanes(chunk))
        return remote(spat.at[part], recv.at[part], m_ss.at[chunk], m_rs.at[chunk], tm=prev_id)

    def give(chunk):
        part = (slice(None), slice(None), lanes(chunk))
        return remote(outs.at[part], out_ref.at[part], o_ss.at[chunk], o_rs.at[chunk], tm=next_id)

    def finish_attention():
        for off in range(1, n_sp):
            gather(off).wait_recv()
        for t in range(heads_tiles):
            owner, local = t // per, t % per
            tile = prefix[local]
            for off in range(1, n_sp):
                tile = jnp.where(lax.rem(s + n_sp - off, n_sp) == owner, full[off - 1, local], tile)
            big = jnp.concatenate([tile[:HEAD_DIM]] * (LANES // HEAD_DIM), axis=0)
            keys = jnp.broadcast_to(tile[HEAD_DIM : HEAD_DIM + 1], (LANES, LANES)).T
            both = jnp.concatenate([jnp.where(same, big, 0.0), jnp.where(same, keys, 0.0)], axis=1)
            high = both.astype(BF16)
            low = (both - high.astype(F32)).astype(BF16)
            query = jnp.maximum(tile_of(q_ref, t), 0.0).astype(BF16)
            got = jnp.dot(query, high, preferred_element_type=F32) + jnp.dot(query, low, preferred_element_type=F32)
            value = (got[:, :LANES] / (got[:, LANES:] + 1.0)).astype(BF16)
            lo, hi = t * LANES, min(channels, (t + 1) * LANES)
            att_ref[:, lo:hi] = value[:, : hi - lo]

    sent_back = 0
    for place, chunk in enumerate(order):
        for side, cond in ((0, has_up), (1, has_down)):
            when(cond)(lambda chunk=chunk, side=side: halo_in(chunk, side).wait_recv())
        conv(chunk)
        if chunk in a_list:
            when(has_next)(lambda chunk=chunk: ahead(chunk).start())
        elif sent_back < 2:
            when(has_prev)(lambda chunk=chunk: back(chunk).start())
            sent_back += 1
        if place == 0:
            for off in range(1, n_sp):
                scatter(off).wait_recv()
            when(c == 0)(hop)

    @when(jnp.logical_not(has_prev))
    def _():
        for chunk in a_list:
            gate(chunk, None, spat, out_ref)

    for i, chunk in enumerate(b_list):
        @when(jnp.logical_not(has_prev))
        def _():
            gate(chunk, None, spat, out_ref)

        @when(has_next)
        def _():
            back(chunk).wait_recv()
            gate(chunk, spat, recv, outs)
            give(chunk).start()

        @when(has_prev)
        def _():
            back(chunk).wait_send()
            if i + 2 < len(b_list):
                back(b_list[i + 2]).start()

        last = i == max(0, len(b_list) - 2)
        if last:
            when(jnp.logical_and(has_prev, c >= i + 1))(hop)
            finish_attention()
        elif i < len(b_list) - 2:
            when(c == i + 1)(hop)
        if i >= 2 and i - 2 < len(a_list) - 1 and i < len(b_list) - 1:
            @when(has_prev)
            def _():
                ahead(a_list[i - 2]).wait_recv()
                gate(a_list[i - 2], recv, spat, out_ref)

    done = len([i for i in range(len(b_list)) if i >= 2 and i - 2 < len(a_list) - 1 and i < len(b_list) - 1])

    @when(has_prev)
    def _():
        for chunk in a_list[done:]:
            ahead(chunk).wait_recv()
            gate(chunk, recv, spat, out_ref)
        for chunk in b_list:
            give(chunk).wait_recv()

    @when(has_next)
    def _():
        for chunk in a_list:
            ahead(chunk).wait_send()
        for chunk in b_list:
            give(chunk).wait_send()
        chain().wait_send()

    for off in range(1, n_sp):
        scatter(off).wait_send()
        gather(off).wait_send()
    for chunk in order:
        for way, cond in ((0, has_up), (1, has_down)):
            when(cond)(lambda chunk=chunk, way=way: halo(chunk, way).wait_send())


def plan_of(n_tm, n_sp, chunks):
    n_a = max(1, round(chunks / 3))
    a_list = list(range(n_a))
    b_list = list(range(n_a, chunks))
    order = []
    for i in range(max(len(a_list), len(b_list))):
        order += b_list[i : i + 1] + a_list[i : i + 1]
    return n_tm, n_sp, order, a_list, b_list


def on_device(query_proj, key_proj, value_proj, expanded, spatial_weight, temporal_weight):
    n_tm, n_sp = lax.axis_size("tm"), lax.axis_size("space")
    frames, rows, cols, channels = query_proj.shape
    hidden = expanded.shape[-1]
    chunks = -(-hidden // (CHUNK * LANES))
    padded = chunks * CHUNK * LANES
    extra = padded - hidden
    tokens = frames * rows * cols
    x = jnp.pad(expanded.transpose(3, 0, 1, 2, 4), ((0, 0),) * 4 + ((0, extra),))
    x = x.reshape(2, frames, rows * cols, padded)
    sw = jnp.pad(spatial_weight, ((0, 0),) * 3 + ((0, extra),))
    tw = jnp.pad(temporal_weight, ((0, 0),) * 2 + ((0, extra),))
    per = -(-(-(-channels // LANES)) // n_sp)
    dma = pltpu.SemaphoreType.DMA
    vmem = pl.BlockSpec(memory_space=pltpu.VMEM)
    att, out = pl.pallas_call(
        functools.partial(kernel, plan_of(n_tm, n_sp, chunks)),
        out_shape=(
            jax.ShapeDtypeStruct((tokens, channels), BF16),
            jax.ShapeDtypeStruct((frames, rows * cols, padded), BF16),
        ),
        in_specs=[vmem] * 6,
        out_specs=(vmem, vmem),
        scratch_shapes=[
            pltpu.VMEM((2, frames, rows * cols, padded), BF16),
            pltpu.VMEM((2, frames, rows * cols, padded), BF16),
            pltpu.VMEM((frames, rows * cols, padded), BF16),
            pltpu.VMEM((2, 2, frames * cols, padded), BF16),
            pltpu.VMEM((2, 2, frames * cols, padded), BF16),
            pltpu.VMEM((per * n_sp, ST, LANES), F32),
            pltpu.VMEM((n_sp - 1, per, ST, LANES), F32),
            pltpu.VMEM((per, ST, LANES), F32),
            pltpu.VMEM((per, ST, LANES), F32),
            pltpu.VMEM((n_sp - 1, per, ST, LANES), F32),
            dma((2, chunks)), dma((2, chunks)),
            dma((chunks,)), dma((chunks,)),
            dma((chunks,)), dma((chunks,)),
            dma((n_sp - 1,)), dma((n_sp - 1,)),
            dma((n_sp - 1,)), dma((n_sp - 1,)),
            dma, dma,
        ],
        compiler_params=pltpu.CompilerParams(
            collective_id=0, has_side_effects=True, vmem_limit_bytes=40 * 1024 * 1024
        ),
    )(
        query_proj.reshape(tokens, channels),
        key_proj.reshape(tokens, channels),
        value_proj.reshape(tokens, channels),
        x, sw, tw,
    )
    attended = att.reshape(frames, rows, cols, channels)
    gated = out.reshape(frames, rows, cols, padded)[..., :hidden]
    return attended, gated


def solution(mesh):
    token = P(("groups", "tm"), "space", None, "mp")
    return jax.shard_map(
        on_device,
        mesh=mesh,
        in_specs=(
            token, token, token,
            P(("groups", "tm"), "space", None, None, "mp"),
            P(None, None, None, "mp"),
            P(None, None, "mp"),
        ),
        out_specs=(token, token),
        check_vma=False,
    )
```

time: 115 us -> 48 us (0.42)
  the two profiles are of different devices: /device:TPU:0 before, /device:TPU:24 now
where the time goes in v1:
time: 48 us; the launch traced here: 47.8 us
  Pallas kernels  42.5 us (89%)
  local copies, waits for them, and re-layouts  4.54 us (9%)
  between operations  0.71 us (1%)
    pallas_call x1, Pallas kernels, on_device(): pl.pallas_call(functools.partial(kernel, plan_of(n_tm, n_sp, chunks)), ou...  42.5 us
    unnamed x13, local copies, waits for them, and re-layouts  4.29 us

profile of v1, /device:TPU:24, one launch (start us, length us, event | category | flops | bytes accessed | tf_op | source)
XLA Modules:
  0.0 47.8 jit_solution(8645544950088190638)
XLA Ops:
  0.6 1.7 %copy.9 = bf16[2,2,8,8,3360]{4,3,2,1,0:T(8,128)(2,1)S(1)} copy(bf16[2,2,8,8,3360]{4,0,3,2,1:T(2,128)(2,1)} %bitcast.14) | data formatting | bytes 3440640
  2.3 0.0 copy-start.3
  2.3 0.0 copy-start.4
  2.3 0.0 copy-start
  2.3 0.0 copy-start.1
  2.3 0.0 copy-start.2
  2.3 0.1 pad_bitcast_fusion.x_ref
  2.5 0.8 %copy-done.3 = f32[3,3,2,3360]{3,2,1,0:T(2,128)S(1)} copy-done((f32[3,3,2,3360]{3,2,1,0:T(2,128)S(1)}, f32[3,3,2,3360]{3,2,1,0:T(2,128)}, u32[]{:S(2)}) %copy-start.3) | copy-done | bytes 241944
  3.2 0.1 pad.13.sw_ref
  3.3 0.0 copy-done.4
  3.4 0.1 copy-done
  3.4 0.1 copy-done.1
  3.5 0.1 copy-done.2
  3.6 42.5 %shard_map.77 = (bf16[128,1120]{1,0:T(8,128)(2,1)S(1)}, bf16[2,64,3456]{2,1,0:T(8,128)(2,1)S(1)}) custom-call(bf16[128,1120]{1,0:T(8,128)(2,1)S(1)} %bitcast.10, bf16[128,1120]{1,0:T(8,128)(2,1)S(1)} %bitcast.11, bf16[128,1120]{1,0:T(8,128)(2,1)S(1)} %bitcast.12, bf16[2,2,64,3456]{3,2,1,0:T(8,128)(2,1)S(1)} %pad_bitcast_fusion.x_ref, ...), custom_call_target="tpu_custom_call" | custom-call | tf_op jit(solution)/shard_map/pallas_call | solution.py:355
  46.2 0.7 %copy.12 = bf16[2,8,8,1120]{3,2,1,0:T(8,128)(2,1)} copy(bf16[2,8,8,1120]{3,2,1,0:T(8,128)(2,1)S(1)} %bitcast.13) | data formatting | bytes 573440
  46.9 0.9 %copy.13 = bf16[2,8,8,3360]{3,2,1,0:T(8,128)(2,1)} copy(bf16[2,8,8,3360]{3,2,1,0:T(8,128)(2,1)S(1)} %bitcast.9) | data formatting | bytes 1720320
  (1 shorter events, 0.0 us)
Async XLA Ops:
  2.3 0.9 %copy-start.3 = (f32[3,3,2,3360]{3,2,1,0:T(2,128)S(1)}, f32[3,3,2,3360]{3,2,1,0:T(2,128)}, u32[]{:S(2)}) copy-start(f32[3,3,2,3360]{3,2,1,0:T(2,128)} %param.10) | copy-start | bytes 725764
  2.3 1.0 %copy-start.4 = (f32[3,2,3360]{2,1,0:T(2,128)S(1)}, f32[3,2,3360]{2,1,0:T(2,128)}, u32[]{:S(2)}) copy-start(f32[3,2,3360]{2,1,0:T(2,128)} %param.11) | copy-start | bytes 241924
  2.3 1.1 %copy-start = (bf16[2,8,8,1120]{3,2,1,0:T(8,128)(2,1)S(1)}, bf16[2,8,8,1120]{3,2,1,0:T(8,128)(2,1)}, u32[]{:S(2)}) copy-start(bf16[2,8,8,1120]{3,2,1,0:T(8,128)(2,1)} %param.6) | copy-start | bytes 860164
  2.3 1.2 %copy-start.1 = (bf16[2,8,8,1120]{3,2,1,0:T(8,128)(2,1)S(1)}, bf16[2,8,8,1120]{3,2,1,0:T(8,128)(2,1)}, u32[]{:S(2)}) copy-start(bf16[2,8,8,1120]{3,2,1,0:T(8,128)(2,1)} %param.7) | copy-start | bytes 860164
  2.3 1.3 %copy-start.2 = (bf16[2,8,8,1120]{3,2,1,0:T(8,128)(2,1)S(1)}, bf16[2,8,8,1120]{3,2,1,0:T(8,128)(2,1)}, u32[]{:S(2)}) copy-start(bf16[2,8,8,1120]{3,2,1,0:T(8,128)(2,1)} %param.8) | copy-start | bytes 860164

commit v2 on v1

--- a/solution.py
+++ b/solution.py
@@ -9,7 +9,12 @@
 
 HEAD_DIM = 32
 LANES = 128
-CHUNK = 3
+EARLY = 4
+LATE = 3
+CHUNK = 4
+A_SHARE = 1 / 3
+B_CHUNK = 4
+AHEAD = 4
 ST = HEAD_DIM + 8
 MESH = pl.DeviceIdType.MESH
 F32 = jnp.float32
@@ -21,7 +26,7 @@
     spat, recv, outs, hsend, hrecv, state, rs_buf, prefix, pre_in, full,
     h_ss, h_rs, m_ss, m_rs, o_ss, o_rs, rs_ss, rs_rs, ag_ss, ag_rs, ch_ss, ch_rs,
 ):
-    n_tm, n_sp, order, a_list, b_list = plan
+    n_tm, n_sp, order, a_list, b_list, spans = plan
     frames = x_ref.shape[1]
     cols = hsend.shape[2] // frames
     rows = x_ref.shape[2] // cols
@@ -29,10 +34,9 @@
     s = lax.axis_index("space")
     has_prev, has_next = c > 0, c < n_tm - 1
     has_up, has_down = s > 0, s < n_sp - 1
-    width = CHUNK * LANES
 
     def lanes(chunk):
-        return pl.ds(chunk * width, width)
+        return pl.ds(spans[chunk][0] * LANES, spans[chunk][1] * LANES)
 
     def remote(src, dst, ss, rs, **where):
         return pltpu.make_async_remote_copy(
@@ -58,7 +62,6 @@
     def _():
         pl.semaphore_signal(barrier, inc=1, device_id={"tm": next_id}, device_id_type=MESH)
 
-    n_tiles = x_ref.shape[3] // LANES
 
     def edges(t, _):
         at = pl.ds(pl.multiple_of(t * LANES, LANES), LANES)
@@ -69,7 +72,11 @@
             hsend[1, vg, :, at] = jnp.concatenate(low, axis=0).astype(BF16)
         return 0
 
-    lax.fori_loop(0, n_tiles, edges, 0)
+    def edges_of(chunk):
+        lax.fori_loop(spans[chunk][0], sum(spans[chunk]), edges, 0)
+
+    for chunk in order[:EARLY]:
+        edges_of(chunk)
 
     @when(jnp.logical_not(has_up))
     def _():
@@ -93,9 +100,15 @@
             h_ss.at[side, chunk], h_rs.at[side, chunk], space=up_id if side == 0 else down_id,
         )
 
-    for chunk in order:
+    def send_edges(chunk):
         for way, cond in ((0, has_up), (1, has_down)):
-            when(cond)(lambda chunk=chunk, way=way: halo(chunk, way).start())
+            when(cond)(lambda way=way: halo(chunk, way).start())
+
+    for chunk in order[:EARLY]:
+        send_edges(chunk)
+    for chunk in order[EARLY:]:
+        edges_of(chunk)
+        send_edges(chunk)
 
     channels = q_ref.shape[-1]
     heads_tiles = -(-channels // LANES)
@@ -111,20 +124,21 @@
             part = jnp.concatenate([part, jnp.zeros((tokens, LANES - hi + lo), F32)], axis=1)
         return part
 
-    for t in range(heads_tiles):
-        key = jnp.maximum(tile_of(k_ref, t), 0.0)
-        kv = lax.dot_general(
-            key.T.astype(BF16), tile_of(v_ref, t).astype(BF16),
-            (((1,), (0,)), ((), ())), preferred_element_type=F32,
-        )
-        kv = jnp.where(same, kv, 0.0)
-        small = kv[:HEAD_DIM]
-        for j in range(1, LANES // HEAD_DIM):
-            small = small + kv[j * HEAD_DIM : (j + 1) * HEAD_DIM]
-        state[t, :HEAD_DIM] = small
-        state[t, HEAD_DIM:] = jnp.broadcast_to(jnp.sum(key, axis=0, keepdims=True), (ST - HEAD_DIM, LANES))
-    for t in range(heads_tiles, state.shape[0]):
-        state[t] = jnp.zeros((ST, LANES), F32)
+    def local_state():
+        for t in range(heads_tiles):
+            key = jnp.maximum(tile_of(k_ref, t), 0.0)
+            kv = lax.dot_general(
+                key.T.astype(BF16), tile_of(v_ref, t).astype(BF16),
+                (((1,), (0,)), ((), ())), preferred_element_type=F32,
+            )
+            kv = jnp.where(same, kv, 0.0)
+            small = kv[:HEAD_DIM]
+            for j in range(1, LANES // HEAD_DIM):
+                small = small + kv[j * HEAD_DIM : (j + 1) * HEAD_DIM]
+            state[t, :HEAD_DIM] = small
+            state[t, HEAD_DIM:] = jnp.broadcast_to(jnp.sum(key, axis=0, keepdims=True), (ST - HEAD_DIM, LANES))
+        for t in range(heads_tiles, state.shape[0]):
+            state[t] = jnp.zeros((ST, LANES), F32)
 
     per = state.shape[0] // n_sp
 
@@ -139,8 +153,6 @@
         peer = lax.rem(s + off, n_sp)
         return remote(prefix, full.at[off - 1], ag_ss.at[off - 1], ag_rs.at[off - 1], space=peer)
 
-    for off in range(1, n_sp):
-        scatter(off).start()
 
     def chain():
         return remote(prefix, pre_in, ch_ss, ch_rs, tm=next_id)
@@ -167,7 +179,7 @@
 
     def conv(chunk):
         def tile(t, _):
-            at = pl.ds(pl.multiple_of(chunk * width + t * LANES, LANES), LANES)
+            at = pl.ds(pl.multiple_of((spans[chunk][0] + t) * LANES, LANES), LANES)
             for vg in range(2):
                 taps = []
                 for a in range(3):
@@ -192,11 +204,11 @@
                     spat[vg, f, :, at] = total.reshape(rows * cols, LANES).astype(BF16)
             return 0
 
-        lax.fori_loop(0, CHUNK, tile, 0)
+        lax.fori_loop(0, spans[chunk][1], tile, 0)
 
     def gate(chunk, before, now, into):
         def tile(t, _):
-            at = pl.ds(pl.multiple_of(chunk * width + t * LANES, LANES), LANES)
+            at = pl.ds(pl.multiple_of((spans[chunk][0] + t) * LANES, LANES), LANES)
             mixed = []
             for vg in range(2):
                 w = [tw_ref[j, vg : vg + 1, at] for j in range(3)]
@@ -219,7 +231,7 @@
                 into[f, :, at] = (v * (g / (1.0 + jnp.exp(-g)))).astype(BF16)
             return 0
 
-        lax.fori_loop(0, CHUNK, tile, 0)
+        lax.fori_loop(0, spans[chunk][1], tile, 0)
 
     def ahead(chunk):
         part = (slice(None), slice(None), slice(None), lanes(chunk))
@@ -257,12 +269,16 @@
         for side, cond in ((0, has_up), (1, has_down)):
             when(cond)(lambda chunk=chunk, side=side: halo_in(chunk, side).wait_recv())
         conv(chunk)
-        if chunk in a_list:
+        if chunk in a_list[:2]:
             when(has_next)(lambda chunk=chunk: ahead(chunk).start())
-        elif sent_back < 2:
+        elif chunk in b_list and sent_back < AHEAD:
             when(has_prev)(lambda chunk=chunk: back(chunk).start())
             sent_back += 1
-        if place == 0:
+        if place == min(LATE, len(order) - 1):
+            local_state()
+            for off in range(1, n_sp):
+                scatter(off).start()
+        if place == min(LATE + 1, len(order) - 1):
             for off in range(1, n_sp):
                 scatter(off).wait_recv()
             when(c == 0)(hop)
@@ -272,6 +288,9 @@
         for chunk in a_list:
             gate(chunk, None, spat, out_ref)
 
+    for chunk in a_list[len(b_list) + 1 :]:
+        when(has_next)(lambda chunk=chunk: ahead(chunk).start())
+    finish = max(1, len(b_list) - 2)
     for i, chunk in enumerate(b_list):
         @when(jnp.logical_not(has_prev))
         def _():
@@ -286,22 +305,23 @@
         @when(has_prev)
         def _():
             back(chunk).wait_send()
-            if i + 2 < len(b_list):
-                back(b_list[i + 2]).start()
-
-        last = i == max(0, len(b_list) - 2)
-        if last:
-            when(jnp.logical_and(has_prev, c >= i + 1))(hop)
+            if i + AHEAD < len(b_list):
+                back(b_list[i + AHEAD]).start()
+
+        if 2 <= i + 1 < len(a_list):
+            when(has_next)(lambda i=i: ahead(a_list[i + 1]).start())
+        if i == finish:
+            when(jnp.logical_and(has_prev, c >= i))(hop)
             finish_attention()
-        elif i < len(b_list) - 2:
-            when(c == i + 1)(hop)
-        if i >= 2 and i - 2 < len(a_list) - 1 and i < len(b_list) - 1:
+        elif 1 <= i < finish:
+            when(c == i)(hop)
+        if 2 <= i < len(b_list) - 1 and i - 2 < len(a_list):
             @when(has_prev)
             def _():
                 ahead(a_list[i - 2]).wait_recv()
                 gate(a_list[i - 2], recv, spat, out_ref)
 
-    done = len([i for i in range(len(b_list)) if i >= 2 and i - 2 < len(a_list) - 1 and i < len(b_list) - 1])
+    done = max(0, min(len(a_list), len(b_list) - 3))
 
     @when(has_prev)
     def _():
@@ -327,22 +347,34 @@
             when(cond)(lambda chunk=chunk, way=way: halo(chunk, way).wait_send())
 
 
-def plan_of(n_tm, n_sp, chunks):
-    n_a = max(1, round(chunks / 3))
-    a_list = list(range(n_a))
-    b_list = list(range(n_a, chunks))
+def cut(total, most):
+    count = -(-total // most)
+    return [total // count + (1 if i < total % count else 0) for i in range(count)]
+
+
+def plan_of(n_tm, n_sp, tiles):
+    forward = max(1, round(tiles * A_SHARE))
+    a_sizes = [1] + cut(forward - 1, CHUNK) if forward > 1 else [forward]
+    rest = tiles - forward
+    b_sizes = [1, 2] + cut(rest - 6, B_CHUNK) + [2, 1] if rest >= 8 else [1] * rest
+    spans, at = [], 0
+    for size in a_sizes + b_sizes:
+        spans.append((at, size))
+        at += size
+    a_list = list(range(len(a_sizes)))
+    b_list = list(range(len(a_sizes), len(spans)))
     order = []
     for i in range(max(len(a_list), len(b_list))):
         order += b_list[i : i + 1] + a_list[i : i + 1]
-    return n_tm, n_sp, order, a_list, b_list
+    return n_tm, n_sp, order, a_list, b_list, spans
 
 
 def on_device(query_proj, key_proj, value_proj, expanded, spatial_weight, temporal_weight):
     n_tm, n_sp = lax.axis_size("tm"), lax.axis_size("space")
     frames, rows, cols, channels = query_proj.shape
     hidden = expanded.shape[-1]
-    chunks = -(-hidden // (CHUNK * LANES))
-    padded = chunks * CHUNK * LANES
+    tiles = -(-hidden // LANES)
+    padded = tiles * LANES
     extra = padded - hidden
     tokens = frames * rows * cols
     x = jnp.pad(expanded.transpose(3, 0, 1, 2, 4), ((0, 0),) * 4 + ((0, extra),))
@@ -350,10 +382,12 @@
     sw = jnp.pad(spatial_weight, ((0, 0),) * 3 + ((0, extra),))
     tw = jnp.pad(temporal_weight, ((0, 0),) * 2 + ((0, extra),))
     per = -(-(-(-channels // LANES)) // n_sp)
+    plan = plan_of(n_tm, n_sp, tiles)
+    chunks = len(plan[-1])
     dma = pltpu.SemaphoreType.DMA
     vmem = pl.BlockSpec(memory_space=pltpu.VMEM)
     att, out = pl.pallas_call(
-        functools.partial(kernel, plan_of(n_tm, n_sp, chunks)),
+        functools.partial(kernel, plan),
         out_shape=(
             jax.ShapeDtypeStruct((tokens, channels), BF16),
             jax.ShapeDtypeStruct((frames, rows * cols, padded), BF16),

time: 48 us -> 40.5 us (0.84)
  the two profiles are of different devices: /device:TPU:24 before, /device:TPU:0 now
where the time goes in v2:
time: 40.5 us; the launch traced here: 40.4 us
  Pallas kernels  35.1 us (87%)
  local copies, waits for them, and re-layouts  4.54 us (11%)
  between operations  0.71 us (2%)
    pallas_call x1, Pallas kernels, on_device(): pl.pallas_call(functools.partial(kernel, plan), out_shape=(jax.ShapeDtype...  35.1 us
    unnamed x13, local copies, waits for them, and re-layouts  4.29 us

profile of v2, /device:TPU:0, one launch (start us, length us, event | category | flops | bytes accessed | tf_op | source)
XLA Modules:
  0.0 40.4 jit_solution(1623049889134442038)
XLA Ops:
  0.6 1.7 %copy.9 = bf16[2,2,8,8,3360]{4,3,2,1,0:T(8,128)(2,1)S(1)} copy(bf16[2,2,8,8,3360]{4,0,3,2,1:T(2,128)(2,1)} %bitcast.14) | data formatting | bytes 3440640
  2.3 0.0 copy-start.3
  2.3 0.0 copy-start.4
  2.3 0.0 copy-start
  2.3 0.0 copy-start.1
  2.3 0.0 copy-start.2
  2.3 0.1 pad_bitcast_fusion.x_ref
  2.5 0.8 %copy-done.3 = f32[3,3,2,3360]{3,2,1,0:T(2,128)S(1)} copy-done((f32[3,3,2,3360]{3,2,1,0:T(2,128)S(1)}, f32[3,3,2,3360]{3,2,1,0:T(2,128)}, u32[]{:S(2)}) %copy-start.3) | copy-done | bytes 241944
  3.2 0.1 pad.13.sw_ref
  3.3 0.0 copy-done.4
  3.4 0.1 copy-done
  3.4 0.1 copy-done.1
  3.5 0.1 copy-done.2
  3.6 35.1 %shard_map.77 = (bf16[128,1120]{1,0:T(8,128)(2,1)S(1)}, bf16[2,64,3456]{2,1,0:T(8,128)(2,1)S(1)}) custom-call(bf16[128,1120]{1,0:T(8,128)(2,1)S(1)} %bitcast.10, bf16[128,1120]{1,0:T(8,128)(2,1)S(1)} %bitcast.11, bf16[128,1120]{1,0:T(8,128)(2,1)S(1)} %bitcast.12, bf16[2,2,64,3456]{3,2,1,0:T(8,128)(2,1)S(1)} %pad_bitcast_fusion.x_ref, ...), custom_call_target="tpu_custom_call" | custom-call | tf_op jit(solution)/shard_map/pallas_call | solution.py:389
  38.7 0.7 %copy.12 = bf16[2,8,8,1120]{3,2,1,0:T(8,128)(2,1)} copy(bf16[2,8,8,1120]{3,2,1,0:T(8,128)(2,1)S(1)} %bitcast.13) | data formatting | bytes 573440
  39.5 0.9 %copy.13 = bf16[2,8,8,3360]{3,2,1,0:T(8,128)(2,1)} copy(bf16[2,8,8,3360]{3,2,1,0:T(8,128)(2,1)S(1)} %bitcast.9) | data formatting | bytes 1720320
  (1 shorter events, 0.0 us)
Async XLA Ops:
  2.3 0.9 %copy-start.3 = (f32[3,3,2,3360]{3,2,1,0:T(2,128)S(1)}, f32[3,3,2,3360]{3,2,1,0:T(2,128)}, u32[]{:S(2)}) copy-start(f32[3,3,2,3360]{3,2,1,0:T(2,128)} %param.10) | copy-start | bytes 725764
  2.3 1.0 %copy-start.4 = (f32[3,2,3360]{2,1,0:T(2,128)S(1)}, f32[3,2,3360]{2,1,0:T(2,128)}, u32[]{:S(2)}) copy-start(f32[3,2,3360]{2,1,0:T(2,128)} %param.11) | copy-start | bytes 241924
  2.3 1.1 %copy-start = (bf16[2,8,8,1120]{3,2,1,0:T(8,128)(2,1)S(1)}, bf16[2,8,8,1120]{3,2,1,0:T(8,128)(2,1)}, u32[]{:S(2)}) copy-start(bf16[2,8,8,1120]{3,2,1,0:T(8,128)(2,1)} %param.6) | copy-start | bytes 860164
  2.3 1.2 %copy-start.1 = (bf16[2,8,8,1120]{3,2,1,0:T(8,128)(2,1)S(1)}, bf16[2,8,8,1120]{3,2,1,0:T(8,128)(2,1)}, u32[]{:S(2)}) copy-start(bf16[2,8,8,1120]{3,2,1,0:T(8,128)(2,1)} %param.7) | copy-start | bytes 860164
  2.3 1.3 %copy-start.2 = (bf16[2,8,8,1120]{3,2,1,0:T(8,128)(2,1)S(1)}, bf16[2,8,8,1120]{3,2,1,0:T(8,128)(2,1)}, u32[]{:S(2)}) copy-start(bf16[2,8,8,1120]{3,2,1,0:T(8,128)(2,1)} %param.8) | copy-start | bytes 860164

commit v3 on v2

--- a/solution.py
+++ b/solution.py
@@ -290,7 +290,7 @@
 
     for chunk in a_list[len(b_list) + 1 :]:
         when(has_next)(lambda chunk=chunk: ahead(chunk).start())
-    finish = max(1, len(b_list) - 2)
+    finish = max(1, len(b_list) - 3)
     for i, chunk in enumerate(b_list):
         @when(jnp.logical_not(has_prev))
         def _():

time: 40.5 us -> 40.5 us (level)
  no operation moved by 1% of the time
where the time goes in v3:
time: 40.5 us; the launch traced here: 40.3 us
  Pallas kernels  35.1 us (87%)
  local copies, waits for them, and re-layouts  4.54 us (11%)
  between operations  0.71 us (2%)
    pallas_call x1, Pallas kernels, on_device(): pl.pallas_call(functools.partial(kernel, plan), out_shape=(jax.ShapeDtype...  35.1 us
    unnamed x13, local copies, waits for them, and re-layouts  4.29 us

profile of v3, /device:TPU:0, one launch (start us, length us, event | category | flops | bytes accessed | tf_op | source)
XLA Modules:
  0.0 40.3 jit_solution(15338234402168468307)
XLA Ops:
  0.6 1.7 %copy.9 = bf16[2,2,8,8,3360]{4,3,2,1,0:T(8,128)(2,1)S(1)} copy(bf16[2,2,8,8,3360]{4,0,3,2,1:T(2,128)(2,1)} %bitcast.14) | data formatting | bytes 3440640
  2.3 0.0 copy-start.3
  2.3 0.0 copy-start.4
  2.3 0.0 copy-start
  2.3 0.0 copy-start.1
  2.3 0.0 copy-start.2
  2.3 0.1 pad_bitcast_fusion.x_ref
  2.5 0.8 %copy-done.3 = f32[3,3,2,3360]{3,2,1,0:T(2,128)S(1)} copy-done((f32[3,3,2,3360]{3,2,1,0:T(2,128)S(1)}, f32[3,3,2,3360]{3,2,1,0:T(2,128)}, u32[]{:S(2)}) %copy-start.3) | copy-done | bytes 241944
  3.2 0.1 pad.13.sw_ref
  3.3 0.0 copy-done.4
  3.4 0.1 copy-done
  3.4 0.1 copy-done.1
  3.5 0.1 copy-done.2
  3.6 35.1 %shard_map.77 = (bf16[128,1120]{1,0:T(8,128)(2,1)S(1)}, bf16[2,64,3456]{2,1,0:T(8,128)(2,1)S(1)}) custom-call(bf16[128,1120]{1,0:T(8,128)(2,1)S(1)} %bitcast.10, bf16[128,1120]{1,0:T(8,128)(2,1)S(1)} %bitcast.11, bf16[128,1120]{1,0:T(8,128)(2,1)S(1)} %bitcast.12, bf16[2,2,64,3456]{3,2,1,0:T(8,128)(2,1)S(1)} %pad_bitcast_fusion.x_ref, ...), custom_call_target="tpu_custom_call" | custom-call | tf_op jit(solution)/shard_map/pallas_call | solution.py:389
  38.7 0.7 %copy.12 = bf16[2,8,8,1120]{3,2,1,0:T(8,128)(2,1)} copy(bf16[2,8,8,1120]{3,2,1,0:T(8,128)(2,1)S(1)} %bitcast.13) | data formatting | bytes 573440
  39.4 0.9 %copy.13 = bf16[2,8,8,3360]{3,2,1,0:T(8,128)(2,1)} copy(bf16[2,8,8,3360]{3,2,1,0:T(8,128)(2,1)S(1)} %bitcast.9) | data formatting | bytes 1720320
  (1 shorter events, 0.0 us)
Async XLA Ops:
  2.3 0.9 %copy-start.3 = (f32[3,3,2,3360]{3,2,1,0:T(2,128)S(1)}, f32[3,3,2,3360]{3,2,1,0:T(2,128)}, u32[]{:S(2)}) copy-start(f32[3,3,2,3360]{3,2,1,0:T(2,128)} %param.10) | copy-start | bytes 725764
  2.3 1.0 %copy-start.4 = (f32[3,2,3360]{2,1,0:T(2,128)S(1)}, f32[3,2,3360]{2,1,0:T(2,128)}, u32[]{:S(2)}) copy-start(f32[3,2,3360]{2,1,0:T(2,128)} %param.11) | copy-start | bytes 241924
  2.3 1.1 %copy-start = (bf16[2,8,8,1120]{3,2,1,0:T(8,128)(2,1)S(1)}, bf16[2,8,8,1120]{3,2,1,0:T(8,128)(2,1)}, u32[]{:S(2)}) copy-start(bf16[2,8,8,1120]{3,2,1,0:T(8,128)(2,1)} %param.6) | copy-start | bytes 860164
  2.3 1.2 %copy-start.1 = (bf16[2,8,8,1120]{3,2,1,0:T(8,128)(2,1)S(1)}, bf16[2,8,8,1120]{3,2,1,0:T(8,128)(2,1)}, u32[]{:S(2)}) copy-start(bf16[2,8,8,1120]{3,2,1,0:T(8,128)(2,1)} %param.7) | copy-start | bytes 860164
  2.3 1.3 %copy-start.2 = (bf16[2,8,8,1120]{3,2,1,0:T(8,128)(2,1)S(1)}, bf16[2,8,8,1120]{3,2,1,0:T(8,128)(2,1)}, u32[]{:S(2)}) copy-start(bf16[2,8,8,1120]{3,2,1,0:T(8,128)(2,1)} %param.8) | copy-start | bytes 860164
